TPU v7x, 256 devices: a whole 4x4x8 slice. The times are simulated.
256 devices in a mesh: site: 64 (over x_lo, z, y), mode: 4 (over x_hi, core).
Axes of the slice: x: 4 (x_hi: 2, x_lo: 2; x = x_hi * 2 + x_lo), y: 4, z: 8, core: 2. Of those that a mesh axis runs over, the one named last changes fastest.
Arguments:
- basis: bfloat16 [512, 400, 512], P('site', 'mode'), may hold values from -6 to 6
- images: bfloat16 [512, 400, 496], P('site', 'mode'), may hold values from -6 to 6
- hops: bfloat16 [512, 9, 400, 400], P('site', None, 'mode'), may hold values from -0.09375 to 0.09375
- neighbours: int32 [512, 8], P('site'), may hold values from 0 to 47, as said below
- rotation: bfloat16 [512, 512], replicated, may hold values from -0.25 to 0.25
Outputs:
- projected: float32 [512, 512], replicated
- rotated_basis: bfloat16 [512, 400, 512], P('site', 'mode')
- rotated_images: bfloat16 [512, 400, 512], P('site', 'mode')
Inputs may be any that keep to these rules, and one draw needn't show every extreme that they name: `neighbours`: the blocks form a periodic 4 x 4 x 4 x 512/64 lattice. Group s = 8 t + 4 gx + 2 gy + gz holds the 2 x 2 x 2 cube of time slice t at spatial offsets 2 gx, 2 gy, 2 gz, stored in its own order.
All inputs are finite; a program needn't handle non-finite values.
Results may differ from a plain program's by a relative error of at most 0.0026.
Values may be sent and summed in bfloat16 or wider, within the bound.
A program may use at most 64 MiB of HBM per device.

v0:
```python
import math

import jax
import jax.numpy as jnp
from jax import lax
from jax.sharding import PartitionSpec as P

OLD = 496


def swapped(block, axis, distance):
    count = lax.axis_size(axis)
    route = []
    for low in range(count):
        high = low | 1 << distance
        if high != low and high < count:
            route += [(low, high), (high, low)]
    return lax.ppermute(block, axis, route)


def from_behind(block, axis, distance):
    devices = range(lax.axis_size(axis))
    route = [((i - distance) % len(devices), i) for i in devices]
    return lax.ppermute(block, axis, route)


def local(basis, images, hops, neighbours, rotation):
    local_blocks = basis.shape[0]
    modes_here = basis.shape[1]
    nvec = basis.shape[2]
    site_count = lax.axis_size("site")
    norm_scale = 1.0 / math.sqrt(site_count * local_blocks * modes_here * lax.axis_size("mode"))
    newest = jnp.transpose(basis[:, :, OLD:], (0, 2, 1))
    pieces = [newest]
    for bit in (2, 1, 0):
        pieces.append(swapped(newest, "site", bit))
    for offset in (-8, 8):
        pieces.append(from_behind(newest, "site", offset))
    stacked = jnp.concatenate(pieces, axis=0)
    widened = lax.all_gather(stacked, "mode", axis=2, tiled=True)
    own_rows = jnp.arange(local_blocks, dtype=jnp.int32)
    row_index = jnp.concatenate([own_rows[:, None], neighbours], axis=1)
    gathered = widened[row_index]
    stencil = jnp.einsum("bdoi,bdki->bok", hops, gathered, preferred_element_type=jnp.float32)
    image_new = stencil.astype(jnp.bfloat16)
    images_all = jnp.concatenate([images, image_new], axis=2)
    full_part = jnp.einsum("bci,bcj->ij", basis, images_all, preferred_element_type=jnp.float32)
    projected = lax.psum(full_part, ("site", "mode")) * norm_scale
    flat_basis = basis.reshape(local_blocks * modes_here, nvec)
    flat_images = images_all.reshape(local_blocks * modes_here, nvec)
    rotated_basis = jnp.dot(flat_basis, rotation, preferred_element_type=jnp.float32).astype(
        jnp.bfloat16
    )
    rotated_images = jnp.dot(flat_images, rotation, preferred_element_type=jnp.float32).astype(
        jnp.bfloat16
    )
    return (
        projected,
        rotated_basis.reshape(local_blocks, modes_here, nvec),
        rotated_images.reshape(local_blocks, modes_here, nvec),
    )


def solution(mesh):
    placed = (
        P("site", "mode", None),
        P("site", "mode", None),
        P("site", None, "mode", None),
        P("site", None),
        P(),
    )
    return jax.shard_map(
        local,
        mesh=mesh,
        in_specs=placed,
        out_specs=(P(), P("site", "mode", None), P("site", "mode", None)),
        check_vma=False,
    )
```

profile of v0, /device:TPU:1, one launch (start us, length us, event | category | flops | bytes accessed | tf_op | source)
XLA Modules:
  0.0 313.2 jit_solution(8573855272539118388)
XLA Ops:
  7.2 0.0 all-reduce.2.cloned.1.call-start
  7.2 1.1 slice.3
  8.4 0.2 copy.47
  8.6 2.5 collective-permute-start
  11.1 2.9 collective-permute-start.1
  14.0 0.4 collective-permute-start.2
  14.4 6.0 %collective-permute-start.3 = (bf16[8,16,100]{2,1,0:T(8,128)(2,1)S(1)}, bf16[8,16,100]{2,1,0:T(8,128)(2,1)S(1)}, u32[]{:S(2)}, u32[]{:S(2)}) collective-permute-start(bf16[8,16,100]{2,1,0:T(8,128)(2,1)S(1)} %bitcast.29), channel_id=1, source_target_pairs={{32,0},{36,4},{40,8},{44,12},{48,16},{52,20},{56,24},{60,28},{64,3... | collective-permute-start | bytes 76808 | tf_op jit(solution)/shard_map/ppermute | solution.py:24
  20.5 0.8 compare_select_fusion
  21.2 0.1 reshape.89
  21.3 1.4 copy.41
  22.7 1.1 copy.39
  23.9 1.0 reshape.83
  25.0 1.2 collective-permute-done.4
  26.3 0.4 copy.36
  26.7 17.3 %all_gather.3 = bf16[48,16,400]{0,1,2:T(8,128)(2,1)S(1)} all-gather(bf16[48,16,100]{0,1,2:T(8,128)(2,1)S(1)} %copy.36), channel_id=1, replica_groups=mesh['site'=64,'mode'=4] {'mode'}, dimensions={2}, use_global_device_ids=true | all-gather | bytes 768000 | tf_op jit(solution)/shard_map/all_gather | solution.py:40
  44.0 2.1 copy.37
  46.1 0.7 gather_fusion
  46.8 5.3 %fusion.8 = bf16[8,100,16]{1,2,0:T(8,128)(2,1)S(1)} fusion(bf16[8,9,16,400]{3,2,1,0:T(8,128)(2,1)S(1)} %bitcast.25, bf16[8,9,100,400]{3,0,2,1:T(8,128)(2,1)} %param.7), kind=kOutput, calls=%fused_computation.8 | convolution fusion | flops 92172800 | bytes 6707200 | tf_op jit(solution)/shard_map/bdoi,bdki->bok/dot_general | solution.py:44
  52.0 0.2 copy.40
  52.2 0.2 pad_maximum_fusion
  52.4 0.8 copy-done.2
  53.2 1.8 convolution_bitcast_fusion
  55.0 0.6 convolution_convert_fusion.1
  55.6 0.1 reshape.84
  55.8 1.1 copy.44
  56.9 0.1 reshape.85
  57.1 0.6 convolution_convert_fusion
  57.7 0.1 reshape.86
  57.8 1.1 copy.45
  59.0 244.8 %all-reduce.2.cloned.1.call-done = f32[512,512]{0,1:T(8,128)} async-done(((f32[512,512]{0,1:T(8,128)}), f32[512,512]{0,1:T(8,128)}) %all-reduce.2.cloned.1.call-update) | async-done | bytes 1048592 | tf_op jit(solution)/shard_map/psum | solution.py:48
  303.7 1.3 broadcast_multiply_fusion
  305.1 1.3 copy.43
  (23 shorter events, 0.1 us)
Async XLA Ops:
  7.2 47.9 %copy-start = (bf16[512,512]{1,0:T(8,128)(2,1)S(1)}, bf16[512,512]{1,0:T(8,128)(2,1)}, u32[]{:S(2)}) copy-start(bf16[512,512]{1,0:T(8,128)(2,1)} %param.9) | copy-start | bytes 1572868
  7.2 15.6 %copy-start.3 = (bf16[8,100,496]{2,0,1:T(8,128)(2,1)S(1)}, bf16[8,100,496]{2,0,1:T(8,128)(2,1)}, u32[]{:S(2)}) copy-start(bf16[8,100,496]{2,0,1:T(8,128)(2,1)} %param.6) | copy-start | bytes 2380804
  7.2 296.5 %all-reduce.2.cloned.1.call-start = ((), (), s32[]{:S(2)}) async-start(), calls=%async_computation | async-start | bytes 2097152 | tf_op jit(solution)/shard_map/psum | solution.py:48
  8.6 16.4 %collective-permute-start = (bf16[8,16,100]{2,1,0:T(8,128)(2,1)S(1)}, bf16[8,16,100]{2,1,0:T(8,128)(2,1)S(1)}, u32[]{:S(2)}, u32[]{:S(2)}) collective-permute-start(bf16[8,16,100]{2,1,0:T(8,128)(2,1)S(1)} %bitcast.26), channel_id=1, source_target_pairs={{0,16},{16,0},{4,20},{20,4},{8,24},{24,8},{12,28},{28,12},{32,48},... | collective-permute-start | bytes 76808 | tf_op jit(solution)/shard_map/ppermute | solution.py:18
  11.1 13.8 %collective-permute-start.1 = (bf16[8,16,100]{2,1,0:T(8,128)(2,1)S(1)}, bf16[8,16,100]{2,1,0:T(8,128)(2,1)S(1)}, u32[]{:S(2)}, u32[]{:S(2)}) collective-permute-start(bf16[8,16,100]{2,1,0:T(8,128)(2,1)S(1)} %bitcast.27), channel_id=1, source_target_pairs={{0,8},{8,0},{4,12},{12,4},{16,24},{24,16},{20,28},{28,20},{32,40},... | collective-permute-start | bytes 76808 | tf_op jit(solution)/shard_map/ppermute | solution.py:18
  14.0 10.9 %collective-permute-start.2 = (bf16[8,16,100]{2,1,0:T(8,128)(2,1)S(1)}, bf16[8,16,100]{2,1,0:T(8,128)(2,1)S(1)}, u32[]{:S(2)}, u32[]{:S(2)}) collective-permute-start(bf16[8,16,100]{2,1,0:T(8,128)(2,1)S(1)} %bitcast.28), channel_id=1, source_target_pairs={{0,4},{4,0},{8,12},{12,8},{16,20},{20,16},{24,28},{28,24},{32,36},... | collective-permute-start | bytes 76808 | tf_op jit(solution)/shard_map/ppermute | solution.py:18
  14.4 10.6 %collective-permute-start.3 = (bf16[8,16,100]{2,1,0:T(8,128)(2,1)S(1)}, bf16[8,16,100]{2,1,0:T(8,128)(2,1)S(1)}, u32[]{:S(2)}, u32[]{:S(2)}) collective-permute-start(bf16[8,16,100]{2,1,0:T(8,128)(2,1)S(1)} %bitcast.29), channel_id=1, source_target_pairs={{32,0},{36,4},{40,8},{44,12},{48,16},{52,20},{56,24},{60,28},{64,3... | collective-permute-start | bytes 76808 | tf_op jit(solution)/shard_map/ppermute | solution.py:24
  20.5 5.8 %collective-permute-start.4 = (bf16[8,16,100]{2,1,0:T(8,128)(2,1)S(1)}, bf16[8,16,100]{2,1,0:T(8,128)(2,1)S(1)}, u32[]{:S(2)}, u32[]{:S(2)}) collective-permute-start(bf16[8,16,100]{2,1,0:T(8,128)(2,1)S(1)} %bitcast.30), channel_id=1, source_target_pairs={{224,0},{228,4},{232,8},{236,12},{240,16},{244,20},{248,24},{252,2... | collective-permute-start | bytes 76808 | tf_op jit(solution)/shard_map/ppermute | solution.py:24
  46.8 5.5 %copy-start.1 = (bf16[8,100,496]{2,1,0:T(8,128)(2,1)S(1)}, bf16[8,100,496]{2,1,0:T(8,128)(2,1)}, u32[]{:S(2)}) copy-start(bf16[8,100,496]{2,1,0:T(8,128)(2,1)} %copy.39) | copy-start | bytes 2380804
  52.0 1.2 copy-start.2
  53.2 1.8 copy-start.4
Sparse Core Ops, SparseCore 0:
  55.1 248.5 all-reduce.1
where the time goes:
time: 314 us; the launch traced here: 313 us
  waiting for transfers between devices  246 us (78%)
  blocking collectives  17.3 us (6%)
  between operations  14.2 us (5%)
  local copies, waits for them, and re-layouts  13.3 us (4%)
  starting transfers between devices  11.9 us (4%)
  matrix products  8.25 us (3%)
    psum x1, waiting for transfers between devices, local(): projected = lax.psum(full_part, ('site', 'mode')) * norm_scale  245 us
    all_gather x1, blocking collectives, local(): widened = lax.all_gather(stacked, 'mode', axis=2, tiled=True)  17.3 us
    unnamed x21, local copies, waits for them, and re-layouts  7.14 us
  transfers between devices with their start and end apart: 6, of which 2 were waited for; matrix products, arithmetic and copies ran while one was open for 3% of the time, Pallas kernels for 0%

commit v1 on v0

v1 whole, which is shorter than its diff:
```python
import functools
import math

import jax
import jax.numpy as jnp
from jax import lax
from jax.experimental import pallas as pl
from jax.experimental.pallas import tpu as pltpu
from jax.sharding import PartitionSpec as P

MESH = pl.DeviceIdType.MESH
F32, BF16 = jnp.float32, jnp.bfloat16
PLANE = [(dx, dy) for dx in range(4) for dy in range(4) if dx or dy]
PLANE.sort(key=lambda d: -(min(d[0], 4 - d[0]) + min(d[1], 4 - d[1])))
DEPTH = (4, 3, 5, 2, 6, 1, 7)


def dot(a, b, ca, cb):
    return lax.dot_general(a, b, (((ca,), (cb,)), ((), ())), preferred_element_type=F32)


def iota(shape, dim):
    return lax.broadcasted_iota(jnp.int32, shape, dim)


def kernel(
    scale, basis, images, hops, neighbours, rotation, proj_out, basis_out, images_out,
    a_v, i_v, h_v, r_v, nb_s, piece, wide, gath, part, core_in, half, plane_out, plane_in, depth_buf, gathered,
    rot_part, new_part, new_core, new_plane, new_depth, new_full,
    load_sem, hop_load, halo_send, halo_recv, forward_send, forward_recv, core_sem, plane_send, plane_recv,
    depth_send, depth_recv, gather_send, gather_recv, pass_send, pass_recv,
    ncore_sem, nplane_send, nplane_recv, ndepth_send, ndepth_recv, nlast_sem,
):
    site, mode = lax.axis_index("site"), lax.axis_index("mode")
    y, z, x_lo = site % 4, (site // 4) % 8, site // 32
    core, x_hi = mode % 2, mode // 2
    x = x_hi * 2 + x_lo
    slot = x * 4 + y
    t, r = site // 8, site % 8

    def device(px, py, pz, pc):
        return ((px % 2) * 32 + pz * 4 + py, (px // 2) * 2 + pc)

    other = (site, x_hi * 2 + 1 - core)
    far = (mode + 2) % 4
    mate, far_mate = other[1], (other[1] + 2) % 4
    plane = [((x + dx) % 4, (y + dy) % 4) for dx, dy in PLANE]
    deep = [(z + d) % 8 for d in DEPTH]
    sites = {
        1: t * 8 + (r + 4) % 8,
        2: t * 8 + r // 4 * 4 + (r % 4 + 2) % 4,
        3: t * 8 + r // 2 * 2 + (r + 1) % 2,
        4: ((t + 7) % 8) * 8 + r,
        5: ((t + 1) % 8) * 8 + r,
    }

    loads = [
        pltpu.make_async_copy(src, dst, load_sem.at[n])
        for n, (src, dst) in enumerate(((basis, a_v), (images, i_v), (rotation, r_v), (neighbours, nb_s)))
    ]
    for copy in loads:
        copy.start()
    hop_loads = [pltpu.make_async_copy(hops.at[h], h_v.at[h], hop_load.at[h]) for h in range(9)]
    for copy in hop_loads:
        copy.start()

    barrier = pltpu.get_barrier_semaphore()
    greeted = [other] + [device(px, py, z, core) for px, py in plane] + [device(x, y, pz, core) for pz in deep]
    greeted += [(sites[1], far)] + [(sites[k], m) for k in (4, 5) for m in (mode, far)]
    for peer in greeted:
        pl.semaphore_signal(barrier, inc=1, device_id=peer, device_id_type=MESH)

    def remote(src, dst, send_sem, recv_sem, peer):
        copy = pltpu.make_async_remote_copy(
            src_ref=src, dst_ref=dst, send_sem=send_sem, recv_sem=recv_sem, device_id=peer, device_id_type=MESH
        )
        return copy

    def arrived(dst, send_sem, recv_sem):
        remote(dst, dst, send_sem, recv_sem, other).wait_recv()

    loads[0].wait()
    spread = (
        (iota((128, 128), 0) - 112 == iota((128, 128), 1) % 16) & (iota((128, 128), 0) >= 112)
    ).astype(F32).astype(BF16)
    own_lanes = iota((800, 128), 0) % 8 == iota((800, 128), 1) // 16
    repeated = dot(a_v[:, 384:512], spread, 1, 0)
    repeated = jnp.where(own_lanes, repeated, 0.0).astype(BF16)
    put = (iota((800, 128), 0) // 8 + 100 * mode) % 128 == iota((800, 128), 1)
    piece[0, mode] = dot(repeated, put.astype(F32).astype(BF16), 0, 0).astype(BF16)

    loads[1].wait()
    part[:, 0:384] = dot(a_v[...], i_v[:, 0:384], 0, 0)
    part[:, 384:496] = dot(a_v[...], i_v[:, 384:496], 0, 0)
    part[:, 496:512] = jnp.zeros((512, 16), F32)

    pl.semaphore_wait(barrier, len(greeted))

    sent = []

    def start(copy):
        copy.start()
        sent.append(copy)

    mine = piece.at[0, mode]
    for k, m in ((4, far), (5, far), (4, mode), (5, mode), (2, far), (1, far), (3, far), (0, far), (2, mode), (1, mode), (3, mode)):
        target = site if k == 0 else sites[k]
        start(remote(mine, piece.at[k, mode], halo_send.at[k, m // 2], halo_recv.at[k, mode // 2], (target, m)))
    start(remote(mine, piece.at[0, mode], forward_send.at[0, x_hi], forward_recv.at[0, x_hi], other))
    start(
        remote(
            part.at[pl.ds(256 * (1 - core), 256)], core_in, core_sem.at[0], core_sem.at[1], other
        )
    )

    loads[2].wait()
    basis_out[...] = dot(a_v[...], r_v[...], 1, 0).astype(BF16)

    arrived(core_in, core_sem.at[0], core_sem.at[1])
    summed = part[pl.ds(256 * core, 256), :] + core_in[...]
    for j in range(16):
        half[j] = summed[16 * j : 16 * j + 16]
    plane_out[...] = half[...].astype(BF16)
    for n, (px, py) in enumerate(plane):
        start(remote(plane_out.at[4 * px + py], plane_in.at[n], plane_send.at[n], plane_recv.at[n], device(px, py, z, core)))

    rot_part[...] = dot(i_v[...], r_v[0:496, :], 1, 0)

    for k, m in ((3, mode), (1, mode), (0, far), (2, mode), (3, far), (1, far), (2, far), (4, mode), (5, mode), (4, far), (5, far)):
        arrived(piece.at[k, m], halo_send.at[k, m // 2], halo_recv.at[k, m // 2])
        start(remote(piece.at[k, m], piece.at[k, m], forward_send.at[k, m // 2], forward_recv.at[k, m // 2], other))

    lane = iota((8, 16, 128), 2)
    for k in range(6):
        for m in (mate, far_mate):
            arrived(piece.at[k, m], forward_send.at[k, m // 2], forward_recv.at[k, m // 2])
        p0, p1, p2, p3 = (piece[k, m] for m in range(4))
        rows = pl.ds(8 * k, 8)
        p0, p1, p2, p3 = (p.reshape(8, 16, 128) for p in (p0, p1, p2, p3))
        wide[rows, :, 0:128] = jnp.where(lane < 100, p0, p1)
        wide[rows, :, 128:256] = jnp.where(lane < 72, p1, p2)
        wide[rows, :, 256:384] = jnp.where(lane < 44, p2, p3)
        wide[rows, :, 384:512] = p3

    for n in range(15):
        arrived(plane_in.at[n], plane_send.at[n], plane_recv.at[n])
    total = half[slot]
    for n in range(15):
        total = total + plane_in[n].astype(F32)
    depth_buf[z] = total
    for n, pz in enumerate(deep):
        start(remote(depth_buf.at[z], depth_buf.at[z], depth_send.at[n], depth_recv.at[z], device(x, y, pz, core)))

    loads[3].wait()
    for h in range(9):
        for b in range(8):
            e = b if h == 0 else nb_s[b, h - 1]
            gath[h, 16 * b : 16 * b + 16, :] = wide[e]
    image = None
    for h in range(9):
        hop_loads[h].wait()
        term = dot(h_v[h], gath[h, :, 0:400], 1, 1)
        image = term if image is None else image + term
    image = jnp.where(own_lanes, image, 0.0).astype(BF16)

    by_block = dot(image, a_v[...], 0, 0)
    new = by_block[0:16]
    for b in range(1, 8):
        new = new + by_block[16 * b : 16 * b + 16]
    new_part[0] = new[:, 0:256]
    new_part[1] = new[:, 256:512]
    start(remote(new_part.at[1 - core], new_core, ncore_sem.at[0], ncore_sem.at[1], other))

    last = jnp.concatenate([r_v[496:512, :]] * 8, axis=0)
    images_out[...] = (rot_part[...] + dot(image, last, 1, 0)).astype(BF16)

    arrived(new_core, ncore_sem.at[0], ncore_sem.at[1])
    new_plane[slot] = (new_part[core] + new_core[...]).astype(BF16)
    for n, (px, py) in enumerate(plane):
        start(remote(new_plane.at[slot], new_plane.at[slot], nplane_send.at[n], nplane_recv.at[slot], device(px, py, z, core)))

    for pz in deep:
        arrived(depth_buf.at[pz], depth_send.at[0], depth_recv.at[pz])
    total = depth_buf[0]
    for n in range(1, 8):
        total = total + depth_buf[n]
    gathered[16 * core + slot] = (total * scale).astype(BF16)
    own = gathered.at[16 * core + slot]
    for n, (px, py) in enumerate(plane):
        start(remote(own, own, gather_send.at[n], gather_recv.at[slot], device(px, py, z, core)))
    start(remote(own, own, pass_send.at[slot], pass_recv.at[slot], other))

    for px, py in plane:
        q = 4 * px + py
        arrived(new_plane.at[q], nplane_send.at[0], nplane_recv.at[q])
    total = new_plane[0].astype(F32)
    for n in range(1, 16):
        total = total + new_plane[n].astype(F32)
    new_depth[z] = total
    for n, pz in enumerate(deep):
        start(remote(new_depth.at[z], new_depth.at[z], ndepth_send.at[n], ndepth_recv.at[z], device(x, y, pz, core)))

    for px, py in plane[::-1]:
        q = 4 * px + py
        block = gathered.at[16 * core + q]
        arrived(block, gather_send.at[0], gather_recv.at[q])
        start(remote(block, block, pass_send.at[q], pass_recv.at[q], other))
    for q in range(16):
        arrived(gathered.at[16 * (1 - core) + q], pass_send.at[0], pass_recv.at[q])
    for q in range(32):
        proj_out[16 * q : 16 * q + 16, :] = gathered[q].astype(F32)

    for pz in deep:
        arrived(new_depth.at[pz], ndepth_send.at[0], ndepth_recv.at[pz])
    total = new_depth[0]
    for n in range(1, 8):
        total = total + new_depth[n]
    new_full[core] = total * scale
    start(remote(new_full.at[core], new_full.at[core], nlast_sem.at[0], nlast_sem.at[1], other))
    arrived(new_full.at[1 - core], nlast_sem.at[0], nlast_sem.at[1])
    for n in range(2):
        proj_out[256 * n : 256 * n + 256, 496:512] = new_full[n].T

    for copy in sent:
        copy.wait_send()


def local(basis, images, hops, neighbours, rotation):
    blocks, modes, nvec = basis.shape
    old = images.shape[2]
    rows = blocks * modes
    sites = lax.axis_size("site") * lax.axis_size("mode")
    scale = 1.0 / math.sqrt(rows * sites)
    flat = lambda v: jnp.transpose(v, (1, 0, 2)).reshape(rows, v.shape[2])
    by_hop = jnp.transpose(hops, (1, 2, 0, 3)).reshape(9, rows, hops.shape[3])
    anywhere = pl.BlockSpec(memory_space=pl.ANY)
    vmem = pl.BlockSpec(memory_space=pltpu.VMEM)
    dma = pltpu.SemaphoreType.DMA
    projected, rotated_basis, rotated_images = pl.pallas_call(
        functools.partial(kernel, scale),
        out_shape=(
            jax.ShapeDtypeStruct((nvec, nvec), F32),
            jax.ShapeDtypeStruct((rows, nvec), BF16),
            jax.ShapeDtypeStruct((rows, nvec), BF16),
        ),
        in_specs=[anywhere] * 5,
        out_specs=(vmem, vmem, vmem),
        scratch_shapes=[
            pltpu.VMEM((rows, nvec), BF16),
            pltpu.VMEM((rows, old), BF16),
            pltpu.VMEM(by_hop.shape, BF16),
            pltpu.VMEM((nvec, nvec), BF16),
            pltpu.SMEM((8, 8), jnp.int32),
            pltpu.VMEM((6, 4, 128, 128), BF16),
            pltpu.VMEM((48, 16, 512), BF16),
            pltpu.VMEM((9, 128, 512), BF16),
            pltpu.VMEM((512, 512), F32),
            pltpu.VMEM((256, 512), F32),
            pltpu.VMEM((16, 16, 512), F32),
            pltpu.VMEM((16, 16, 512), BF16),
            pltpu.VMEM((15, 16, 512), BF16),
            pltpu.VMEM((8, 16, 512), F32),
            pltpu.VMEM((32, 16, 512), BF16),
            pltpu.VMEM((rows, nvec), F32),
            pltpu.VMEM((2, 16, 256), F32),
            pltpu.VMEM((16, 256), F32),
            pltpu.VMEM((16, 16, 256), BF16),
            pltpu.VMEM((8, 16, 256), F32),
            pltpu.VMEM((2, 16, 256), F32),
            dma((4,)),
            dma((9,)),
            dma((6, 2)),
            dma((6, 2)),
            dma((6, 2)),
            dma((6, 2)),
            dma((2,)),
            dma((15,)),
            dma((15,)),
            dma((7,)),
            dma((8,)),
            dma((15,)),
            dma((16,)),
            dma((16,)),
            dma((16,)),
            dma((2,)),
            dma((15,)),
            dma((16,)),
            dma((7,)),
            dma((8,)),
            dma((2,)),
        ],
        compiler_params=pltpu.CompilerParams(
            collective_id=0, has_side_effects=True, vmem_limit_bytes=60 * 2**20
        ),
    )(flat(basis), flat(images), by_hop, neighbours, rotation)
    unflat = lambda v: jnp.transpose(v.reshape(modes, blocks, nvec), (1, 0, 2))
    return projected, unflat(rotated_basis), unflat(rotated_images)


def solution(mesh):
    placed = (
        P("site", "mode", None),
        P("site", "mode", None),
        P("site", None, "mode", None),
        P("site", None),
        P(),
    )
    return jax.shard_map(
        local,
        mesh=mesh,
        in_specs=placed,
        out_specs=(P(), P("site", "mode", None), P("site", "mode", None)),
        check_vma=False,
    )
```

time: 314 us -> 49.6 us (0.16)
  waiting for transfers between devices: 246 us -> 0 us
  Pallas kernels: 0 us -> 42.3 us
  blocking collectives: 17.3 us -> 0 us
  between operations: 14.2 us -> 0.64 us
  starting transfers between devices: 11.9 us -> 0 us
  matrix products: 8.25 us -> 0 us
  local copies, waits for them, and re-layouts: 13.3 us -> 6.44 us
    psum x1 -> x0, waiting for transfers between devices: 245 us -> none  [local(): projected = lax.psum(full_part, ('site', 'mode')) * norm_scale]
    pallas_call x0 -> x1, Pallas kernels: none -> 42.3 us  [local(): pl.pallas_call(functools.partial(kernel, scale), out_shape=(jax.ShapeDtyp...]
    all_gather x1 -> x0, blocking collectives: 17.3 us -> none  [local(): widened = lax.all_gather(stacked, 'mode', axis=2, tiled=True)]
    ppermute x5 -> x0, starting transfers between devices: 11.9 us -> none  [the longest x2 6.05 us: from_behind(): return lax.ppermute(block, axis, route)]
    dot_general x4 -> x0, matrix products: 8.25 us -> none  [the longest x1 5.28 us: local(): jnp.einsum('bdoi,bdki->bok', hops, gathered, preferred_element_type=jnp.f...]
    unnamed x21 -> x3, local copies, waits for them, and re-layouts: 7.14 us -> 6.44 us
  transfers between devices with their start and end apart: 6 -> 0, of which waited for: 2 -> 0; matrix products, arithmetic and copies ran while one was open for 3% -> 0% of each run, Pallas kernels for 0% -> 0%
where the time goes in v1:
time: 49.6 us; the launch traced here: 49.4 us
  Pallas kernels  42.3 us (85%)
  local copies, waits for them, and re-layouts  6.44 us (13%)
  between operations  0.64 us (1%)
    pallas_call x1, Pallas kernels, local(): pl.pallas_call(functools.partial(kernel, scale), out_shape=(jax.ShapeDtyp...  42.3 us
    unnamed x3, local copies, waits for them, and re-layouts  6.44 us

profile of v1, /device:TPU:1, one launch (start us, length us, event | category | flops | bytes accessed | tf_op | source)
XLA Modules:
  0.0 49.4 jit_solution(7440855403921691231)
XLA Ops:
  0.6 42.3 %shard_map.76 = (f32[512,512]{1,0:T(8,128)}, bf16[800,512]{1,0:T(8,128)(2,1)}, bf16[800,512]{1,0:T(8,128)(2,1)}) custom-call(bf16[800,512]{1,0:T(8,128)(2,1)} %bitcast.16, bf16[800,496]{1,0:T(8,128)(2,1)} %bitcast.17, bf16[9,800,400]{2,1,0:T(8,128)(2,1)} %bitcast.15, s32[8,8]{1,0:T(8,128)} %neighbours.1, bf16[512,512]{1,0:T(8,128)(2,1)} %rotation.1), custom_call_target="tpu_custom_call" | custom-call | tf_op jit(solution)/shard_map/pallas_call | solution.py:239
  43.0 2.3 %copy.11 = f32[512,512]{1,0:T(8,128)} copy(f32[512,512]{1,0:T(8,128)} %get-tuple-element.12) | data formatting | bytes 2097152
  45.2 2.1 %copy.12 = bf16[8,100,512]{2,0,1:T(8,128)(2,1)} copy(bf16[8,100,512]{2,0,1:T(8,128)(2,1)} %bitcast.19) | data formatting | bytes 1638400
  47.3 2.1 %copy.13 = bf16[8,100,512]{2,0,1:T(8,128)(2,1)} copy(bf16[8,100,512]{2,0,1:T(8,128)(2,1)} %bitcast.18) | data formatting | bytes 1638400

commit v2 on v1

--- a/solution.py
+++ b/solution.py
@@ -25,11 +25,11 @@
 
 def kernel(
     scale, basis, images, hops, neighbours, rotation, proj_out, basis_out, images_out,
-    a_v, i_v, h_v, r_v, nb_s, piece, wide, gath, part, core_in, half, plane_out, plane_in, depth_buf, gathered,
-    rot_part, new_part, new_core, new_plane, new_depth, new_full,
+    a_v, i_v, h_v, r_v, nb_s, piece, wide, gath, part, image_sum, core_in, half, plane_out, plane_in, depth_buf, gathered,
+    rot_part, new_part, new_core, new_plane, new_depth,
     load_sem, hop_load, halo_send, halo_recv, forward_send, forward_recv, core_sem, plane_send, plane_recv,
     depth_send, depth_recv, gather_send, gather_recv, pass_send, pass_recv,
-    ncore_sem, nplane_send, nplane_recv, ndepth_send, ndepth_recv, nlast_sem,
+    ncore_sem, nplane_send, nplane_recv, ndepth_send, ndepth_recv,
 ):
     site, mode = lax.axis_index("site"), lax.axis_index("mode")
     y, z, x_lo = site % 4, (site // 4) % 8, site // 32
@@ -54,6 +54,12 @@
         5: ((t + 1) % 8) * 8 + r,
     }
 
+    barrier = pltpu.get_barrier_semaphore()
+    greeted = [other] + [device(px, py, z, core) for px, py in plane] + [device(x, y, pz, c) for pz in deep for c in (core, 1 - core)]
+    greeted += [(sites[1], far)] + [(sites[k], m) for k in (4, 5) for m in (mode, far)]
+    for peer in greeted:
+        pl.semaphore_signal(barrier, inc=1, device_id=peer, device_id_type=MESH)
+
     loads = [
         pltpu.make_async_copy(src, dst, load_sem.at[n])
         for n, (src, dst) in enumerate(((basis, a_v), (images, i_v), (rotation, r_v), (neighbours, nb_s)))
@@ -63,12 +69,6 @@
     hop_loads = [pltpu.make_async_copy(hops.at[h], h_v.at[h], hop_load.at[h]) for h in range(9)]
     for copy in hop_loads:
         copy.start()
-
-    barrier = pltpu.get_barrier_semaphore()
-    greeted = [other] + [device(px, py, z, core) for px, py in plane] + [device(x, y, pz, core) for pz in deep]
-    greeted += [(sites[1], far)] + [(sites[k], m) for k in (4, 5) for m in (mode, far)]
-    for peer in greeted:
-        pl.semaphore_signal(barrier, inc=1, device_id=peer, device_id_type=MESH)
 
     def remote(src, dst, send_sem, recv_sem, peer):
         copy = pltpu.make_async_remote_copy(
@@ -126,21 +126,47 @@
 
     rot_part[...] = dot(i_v[...], r_v[0:496, :], 1, 0)
 
-    for k, m in ((3, mode), (1, mode), (0, far), (2, mode), (3, far), (1, far), (2, far), (4, mode), (5, mode), (4, far), (5, far)):
-        arrived(piece.at[k, m], halo_send.at[k, m // 2], halo_recv.at[k, m // 2])
-        start(remote(piece.at[k, m], piece.at[k, m], forward_send.at[k, m // 2], forward_recv.at[k, m // 2], other))
-
     lane = iota((8, 16, 128), 2)
-    for k in range(6):
-        for m in (mate, far_mate):
-            arrived(piece.at[k, m], forward_send.at[k, m // 2], forward_recv.at[k, m // 2])
-        p0, p1, p2, p3 = (piece[k, m] for m in range(4))
-        rows = pl.ds(8 * k, 8)
-        p0, p1, p2, p3 = (p.reshape(8, 16, 128) for p in (p0, p1, p2, p3))
-        wide[rows, :, 0:128] = jnp.where(lane < 100, p0, p1)
-        wide[rows, :, 128:256] = jnp.where(lane < 72, p1, p2)
-        wide[rows, :, 256:384] = jnp.where(lane < 44, p2, p3)
-        wide[rows, :, 384:512] = p3
+
+    def forward(where):
+        for k, m in where:
+            arrived(piece.at[k, m], halo_send.at[k, m // 2], halo_recv.at[k, m // 2])
+            start(remote(piece.at[k, m], piece.at[k, m], forward_send.at[k, m // 2], forward_recv.at[k, m // 2], other))
+
+    def widen(groups):
+        for k in groups:
+            for m in (mate, far_mate):
+                arrived(piece.at[k, m], forward_send.at[k, m // 2], forward_recv.at[k, m // 2])
+            p0, p1, p2, p3 = (piece[k, m].reshape(8, 16, 128) for m in range(4))
+            rows = pl.ds(8 * k, 8)
+            wide[rows, :, 0:128] = jnp.where(lane < 100, p0, p1)
+            wide[rows, :, 128:256] = jnp.where(lane < 72, p1, p2)
+            wide[rows, :, 256:384] = jnp.where(lane < 44, p2, p3)
+            wide[rows, :, 384:512] = p3
+
+    def gather_rows(h):
+        for b in range(8):
+            e = b if h == 0 else nb_s[b, h - 1]
+            gath[h, 16 * b : 16 * b + 16, :] = wide[e]
+
+    def stencil(hs):
+        for h in hs:
+            gather_rows(h)
+            hop_loads[h].wait()
+        for c in range(5):
+            rows = pl.ds(160 * c, 160)
+            term = None if hs[0] == 0 else image_sum[rows, :]
+            for h in hs:
+                product = dot(h_v[h, rows, :], gath[h, :, 0:400], 1, 1)
+                term = product if term is None else term + product
+            image_sum[rows, :] = term
+
+    forward(((3, mode), (1, mode), (0, far), (2, mode), (3, far), (1, far), (2, far)))
+    widen((0, 1, 2, 3))
+    loads[3].wait()
+    stencil((0, 1, 2, 3))
+    forward(((4, mode), (5, mode), (4, far), (5, far)))
+    stencil((4, 5, 6))
 
     for n in range(15):
         arrived(plane_in.at[n], plane_send.at[n], plane_recv.at[n])
@@ -151,17 +177,9 @@
     for n, pz in enumerate(deep):
         start(remote(depth_buf.at[z], depth_buf.at[z], depth_send.at[n], depth_recv.at[z], device(x, y, pz, core)))
 
-    loads[3].wait()
-    for h in range(9):
-        for b in range(8):
-            e = b if h == 0 else nb_s[b, h - 1]
-            gath[h, 16 * b : 16 * b + 16, :] = wide[e]
-    image = None
-    for h in range(9):
-        hop_loads[h].wait()
-        term = dot(h_v[h], gath[h, :, 0:400], 1, 1)
-        image = term if image is None else image + term
-    image = jnp.where(own_lanes, image, 0.0).astype(BF16)
+    widen((4, 5))
+    stencil((7, 8))
+    image = jnp.where(own_lanes, image_sum[...], 0.0).astype(BF16)
 
     by_block = dot(image, a_v[...], 0, 0)
     new = by_block[0:16]
@@ -196,33 +214,47 @@
     total = new_plane[0].astype(F32)
     for n in range(1, 16):
         total = total + new_plane[n].astype(F32)
-    new_depth[z] = total
+    new_depth[core, z] = total.astype(BF16)
+    own = new_depth.at[core, z]
     for n, pz in enumerate(deep):
-        start(remote(new_depth.at[z], new_depth.at[z], ndepth_send.at[n], ndepth_recv.at[z], device(x, y, pz, core)))
-
+        for c in (core, 1 - core):
+            start(remote(own, own, ndepth_send.at[n, c], ndepth_recv.at[core, z], device(x, y, pz, c)))
+    start(remote(own, own, ndepth_send.at[7, 0], ndepth_recv.at[core, z], other))
+
+    def put_out(q):
+        proj_out[pl.ds(pl.multiple_of(16 * q, 16), 16), :] = gathered[q].astype(F32)
+
+    put_out(16 * core + slot)
     for px, py in plane[::-1]:
         q = 4 * px + py
         block = gathered.at[16 * core + q]
         arrived(block, gather_send.at[0], gather_recv.at[q])
         start(remote(block, block, pass_send.at[q], pass_recv.at[q], other))
+        put_out(16 * core + q)
     for q in range(16):
         arrived(gathered.at[16 * (1 - core) + q], pass_send.at[0], pass_recv.at[q])
-    for q in range(32):
-        proj_out[16 * q : 16 * q + 16, :] = gathered[q].astype(F32)
+        put_out(16 * (1 - core) + q)
 
     for pz in deep:
-        arrived(new_depth.at[pz], ndepth_send.at[0], ndepth_recv.at[pz])
-    total = new_depth[0]
-    for n in range(1, 8):
-        total = total + new_depth[n]
-    new_full[core] = total * scale
-    start(remote(new_full.at[core], new_full.at[core], nlast_sem.at[0], nlast_sem.at[1], other))
-    arrived(new_full.at[1 - core], nlast_sem.at[0], nlast_sem.at[1])
-    for n in range(2):
-        proj_out[256 * n : 256 * n + 256, 496:512] = new_full[n].T
+        arrived(new_depth.at[core, pz], ndepth_send.at[0, 0], ndepth_recv.at[core, pz])
+    for pz in [z] + deep:
+        arrived(new_depth.at[1 - core, pz], ndepth_send.at[0, 0], ndepth_recv.at[1 - core, pz])
+    for c in range(2):
+        total = new_depth[c, 0].astype(F32)
+        for n in range(1, 8):
+            total = total + new_depth[c, n].astype(F32)
+        proj_out[256 * c : 256 * c + 256, 496:512] = (total * scale).T
 
     for copy in sent:
         copy.wait_send()
+
+
+def finish(*refs):
+    copies = [pltpu.make_async_copy(refs[n], refs[3 + n], refs[6].at[n]) for n in range(3)]
+    for copy in copies:
+        copy.start()
+    for copy in copies:
+        copy.wait()
 
 
 def local(basis, images, hops, neighbours, rotation):
@@ -233,17 +265,17 @@
     scale = 1.0 / math.sqrt(rows * sites)
     flat = lambda v: jnp.transpose(v, (1, 0, 2)).reshape(rows, v.shape[2])
     by_hop = jnp.transpose(hops, (1, 2, 0, 3)).reshape(9, rows, hops.shape[3])
-    anywhere = pl.BlockSpec(memory_space=pl.ANY)
+    hbm = pl.BlockSpec(memory_space=pltpu.HBM)
     vmem = pl.BlockSpec(memory_space=pltpu.VMEM)
     dma = pltpu.SemaphoreType.DMA
     projected, rotated_basis, rotated_images = pl.pallas_call(
         functools.partial(kernel, scale),
         out_shape=(
-            jax.ShapeDtypeStruct((nvec, nvec), F32),
-            jax.ShapeDtypeStruct((rows, nvec), BF16),
-            jax.ShapeDtypeStruct((rows, nvec), BF16),
+            pltpu.VMEM((nvec, nvec), F32),
+            pltpu.VMEM((rows, nvec), BF16),
+            pltpu.VMEM((rows, nvec), BF16),
         ),
-        in_specs=[anywhere] * 5,
+        in_specs=[hbm] * 5,
         out_specs=(vmem, vmem, vmem),
         scratch_shapes=[
             pltpu.VMEM((rows, nvec), BF16),
@@ -255,6 +287,7 @@
             pltpu.VMEM((48, 16, 512), BF16),
             pltpu.VMEM((9, 128, 512), BF16),
             pltpu.VMEM((512, 512), F32),
+            pltpu.VMEM((rows, 128), F32),
             pltpu.VMEM((256, 512), F32),
             pltpu.VMEM((16, 16, 512), F32),
             pltpu.VMEM((16, 16, 512), BF16),
@@ -265,8 +298,7 @@
             pltpu.VMEM((2, 16, 256), F32),
             pltpu.VMEM((16, 256), F32),
             pltpu.VMEM((16, 16, 256), BF16),
-            pltpu.VMEM((8, 16, 256), F32),
-            pltpu.VMEM((2, 16, 256), F32),
+            pltpu.VMEM((2, 8, 16, 256), BF16),
             dma((4,)),
             dma((9,)),
             dma((6, 2)),
@@ -285,14 +317,25 @@
             dma((2,)),
             dma((15,)),
             dma((16,)),
-            dma((7,)),
-            dma((8,)),
-            dma((2,)),
+            dma((8, 2)),
+            dma((2, 8)),
         ],
         compiler_params=pltpu.CompilerParams(
-            collective_id=0, has_side_effects=True, vmem_limit_bytes=60 * 2**20
+            collective_id=0, has_side_effects=True, vmem_limit_bytes=40 * 2**20
         ),
-    )(flat(basis), flat(images), by_hop, neighbours, rotation)
+    )(*(pltpu.with_memory_space_constraint(v, pltpu.HBM) for v in (flat(basis), flat(images), by_hop, neighbours, rotation)))
+    projected, rotated_basis, rotated_images = pl.pallas_call(
+        finish,
+        out_shape=(
+            jax.ShapeDtypeStruct((nvec, nvec), F32),
+            jax.ShapeDtypeStruct((rows, nvec), BF16),
+            jax.ShapeDtypeStruct((rows, nvec), BF16),
+        ),
+        in_specs=[pl.BlockSpec(memory_space=pl.ANY)] * 3,
+        out_specs=(hbm, hbm, hbm),
+        scratch_shapes=[dma((3,))],
+        compiler_params=pltpu.CompilerParams(vmem_limit_bytes=2**20),
+    )(projected, rotated_basis, rotated_images)
     unflat = lambda v: jnp.transpose(v.reshape(modes, blocks, nvec), (1, 0, 2))
     return projected, unflat(rotated_basis), unflat(rotated_images)
 

time: 49.6 us -> 42.6 us (0.86)
  local copies, waits for them, and re-layouts: 6.44 us -> 0 us
    unnamed x3 -> x0, local copies, waits for them, and re-layouts: 6.44 us -> none
    pallas_call x1 -> x2, Pallas kernels: 42.3 us -> 41.9 us  [the longest x1 40.3 us: local(): pl.pallas_call(functools.partial(kernel, scale), out_shape=(pltpu.VMEM((n...]
where the time goes in v2:
time: 42.6 us; the launch traced here: 42.5 us
  Pallas kernels  41.9 us (98%)
  between operations  0.64 us (2%)
    pallas_call x1, Pallas kernels, local(): pl.pallas_call(functools.partial(kernel, scale), out_shape=(pltpu.VMEM((n...  40.3 us
    pallas_call x1, Pallas kernels, local(): pl.pallas_call(finish, out_shape=(jax.ShapeDtypeStruct((nvec, nvec), F32)...  1.53 us

profile of v2, /device:TPU:1, one launch (start us, length us, event | category | flops | bytes accessed | tf_op | source)
XLA Modules:
  0.0 42.5 jit_solution(2368518540676844568)
XLA Ops:
  0.6 40.3 %shard_map.76 = (f32[512,512]{1,0:T(8,128)S(1)}, bf16[800,512]{1,0:T(8,128)(2,1)S(1)}, bf16[800,512]{1,0:T(8,128)(2,1)S(1)}) custom-call(bf16[800,512]{1,0:T(8,128)(2,1)} %bitcast.16, bf16[800,496]{1,0:T(8,128)(2,1)} %bitcast.17, bf16[9,800,400]{2,1,0:T(8,128)(2,1)} %bitcast.15, s32[8,8]{1,0:T(8,128)} %neighbours.1, bf16[512,512]{1,0:T(8,128)(2,1)} %rotation.1), custom_call_target="tpu_custom_call" | custom-call | tf_op jit(solution)/shard_map/pallas_call | solution.py:271
  41.0 1.5 %shard_map.77 = (f32[512,512]{1,0:T(8,128)}, bf16[800,512]{1,0:T(8,128)(2,1)}, bf16[800,512]{1,0:T(8,128)(2,1)}) custom-call(f32[512,512]{1,0:T(8,128)S(1)} %get-tuple-element.9.refs_0_, bf16[800,512]{1,0:T(8,128)(2,1)S(1)} %get-tuple-element.10.refs_1_, bf16[800,512]{1,0:T(8,128)(2,1)S(1)} %get-tuple-element.11.refs_2_), custom_call_target="tpu_custom_call" | custom-call | tf_op jit(solution)/shard_map/pallas_call | solution.py:327

commit v3 on v2

--- a/solution.py
+++ b/solution.py
@@ -12,6 +12,7 @@
 F32, BF16 = jnp.float32, jnp.bfloat16
 PLANE = [(dx, dy) for dx in range(4) for dy in range(4) if dx or dy]
 PLANE.sort(key=lambda d: -(min(d[0], 4 - d[0]) + min(d[1], 4 - d[1])))
+AWAY = (2, 1, 3, 0)
 DEPTH = (4, 3, 5, 2, 6, 1, 7)
 
 
@@ -27,7 +28,7 @@
     scale, basis, images, hops, neighbours, rotation, proj_out, basis_out, images_out,
     a_v, i_v, h_v, r_v, nb_s, piece, wide, gath, part, image_sum, core_in, half, plane_out, plane_in, depth_buf, gathered,
     rot_part, new_part, new_core, new_plane, new_depth,
-    load_sem, hop_load, halo_send, halo_recv, forward_send, forward_recv, core_sem, plane_send, plane_recv,
+    load_sem, hop_load, halo_send, halo_recv, forward_send, forward_recv, core_send, core_recv, plane_send, plane_recv,
     depth_send, depth_recv, gather_send, gather_recv, pass_send, pass_recv,
     ncore_sem, nplane_send, nplane_recv, ndepth_send, ndepth_recv,
 ):
@@ -66,9 +67,6 @@
     ]
     for copy in loads:
         copy.start()
-    hop_loads = [pltpu.make_async_copy(hops.at[h], h_v.at[h], hop_load.at[h]) for h in range(9)]
-    for copy in hop_loads:
-        copy.start()
 
     def remote(src, dst, send_sem, recv_sem, peer):
         copy = pltpu.make_async_remote_copy(
@@ -90,6 +88,9 @@
     piece[0, mode] = dot(repeated, put.astype(F32).astype(BF16), 0, 0).astype(BF16)
 
     loads[1].wait()
+    hop_loads = [pltpu.make_async_copy(hops.at[h], h_v.at[h], hop_load.at[h]) for h in range(9)]
+    for copy in hop_loads:
+        copy.start()
     part[:, 0:384] = dot(a_v[...], i_v[:, 0:384], 0, 0)
     part[:, 384:496] = dot(a_v[...], i_v[:, 384:496], 0, 0)
     part[:, 496:512] = jnp.zeros((512, 16), F32)
@@ -107,22 +108,27 @@
         target = site if k == 0 else sites[k]
         start(remote(mine, piece.at[k, mode], halo_send.at[k, m // 2], halo_recv.at[k, mode // 2], (target, m)))
     start(remote(mine, piece.at[0, mode], forward_send.at[0, x_hi], forward_recv.at[0, x_hi], other))
-    start(
-        remote(
-            part.at[pl.ds(256 * (1 - core), 256)], core_in, core_sem.at[0], core_sem.at[1], other
-        )
-    )
+    columns = [(x + dx) % 4 for dx in AWAY]
+
+    def quarter(c, px):
+        return pl.ds(pl.multiple_of(256 * c + 64 * px, 64), 64)
+
+    for n, px in enumerate(columns):
+        start(remote(part.at[quarter(1 - core, px)], core_in.at[px], core_send.at[n], core_recv.at[n], other))
 
     loads[2].wait()
     basis_out[...] = dot(a_v[...], r_v[...], 1, 0).astype(BF16)
 
-    arrived(core_in, core_sem.at[0], core_sem.at[1])
-    summed = part[pl.ds(256 * core, 256), :] + core_in[...]
-    for j in range(16):
-        half[j] = summed[16 * j : 16 * j + 16]
-    plane_out[...] = half[...].astype(BF16)
-    for n, (px, py) in enumerate(plane):
-        start(remote(plane_out.at[4 * px + py], plane_in.at[n], plane_send.at[n], plane_recv.at[n], device(px, py, z, core)))
+    for n, px in enumerate(columns):
+        arrived(core_in.at[px], core_send.at[n], core_recv.at[n])
+        summed = part[quarter(core, px), :] + core_in[px]
+        for q in range(4):
+            half[4 * px + q] = summed[16 * q : 16 * q + 16]
+            plane_out[4 * px + q] = summed[16 * q : 16 * q + 16].astype(BF16)
+        for dy in AWAY:
+            if AWAY[n] or dy:
+                py, k = (y + dy) % 4, PLANE.index((AWAY[n], dy))
+                start(remote(plane_out.at[4 * px + py], plane_in.at[k], plane_send.at[k], plane_recv.at[k], device(px, py, z, core)))
 
     rot_part[...] = dot(i_v[...], r_v[0:496, :], 1, 0)
 
@@ -164,10 +170,6 @@
     forward(((3, mode), (1, mode), (0, far), (2, mode), (3, far), (1, far), (2, far)))
     widen((0, 1, 2, 3))
     loads[3].wait()
-    stencil((0, 1, 2, 3))
-    forward(((4, mode), (5, mode), (4, far), (5, far)))
-    stencil((4, 5, 6))
-
     for n in range(15):
         arrived(plane_in.at[n], plane_send.at[n], plane_recv.at[n])
     total = half[slot]
@@ -176,6 +178,10 @@
     depth_buf[z] = total
     for n, pz in enumerate(deep):
         start(remote(depth_buf.at[z], depth_buf.at[z], depth_send.at[n], depth_recv.at[z], device(x, y, pz, core)))
+
+    stencil((0, 1, 2, 3))
+    forward(((4, mode), (5, mode), (4, far), (5, far)))
+    stencil((4, 5, 6))
 
     widen((4, 5))
     stencil((7, 8))
@@ -288,7 +294,7 @@
             pltpu.VMEM((9, 128, 512), BF16),
             pltpu.VMEM((512, 512), F32),
             pltpu.VMEM((rows, 128), F32),
-            pltpu.VMEM((256, 512), F32),
+            pltpu.VMEM((4, 64, 512), F32),
             pltpu.VMEM((16, 16, 512), F32),
             pltpu.VMEM((16, 16, 512), BF16),
             pltpu.VMEM((15, 16, 512), BF16),
@@ -305,7 +311,8 @@
             dma((6, 2)),
             dma((6, 2)),
             dma((6, 2)),
-            dma((2,)),
+            dma((4,)),
+            dma((4,)),
             dma((15,)),
             dma((15,)),
             dma((7,)),

time: 42.6 us -> 40.6 us (0.953)
  Pallas kernels: 41.9 us -> 39.8 us
    pallas_call x1, Pallas kernels: 40.3 us -> 38.3 us  [local(): pl.pallas_call(functools.partial(kernel, scale), out_shape=(pltpu.VMEM((n...]
where the time goes in v3:
time: 40.6 us; the launch traced here: 40.5 us
  Pallas kernels  39.8 us (98%)
  between operations  0.64 us (2%)
    pallas_call x1, Pallas kernels, local(): pl.pallas_call(functools.partial(kernel, scale), out_shape=(pltpu.VMEM((n...  38.3 us
    pallas_call x1, Pallas kernels, local(): pl.pallas_call(finish, out_shape=(jax.ShapeDtypeStruct((nvec, nvec), F32)...  1.53 us

profile of v3, /device:TPU:1, one launch (start us, length us, event | category | flops | bytes accessed | tf_op | source)
XLA Modules:
  0.0 40.5 jit_solution(783061065995008824)
XLA Ops:
  0.6 38.3 %shard_map.76 = (f32[512,512]{1,0:T(8,128)S(1)}, bf16[800,512]{1,0:T(8,128)(2,1)S(1)}, bf16[800,512]{1,0:T(8,128)(2,1)S(1)}) custom-call(bf16[800,512]{1,0:T(8,128)(2,1)} %bitcast.16, bf16[800,496]{1,0:T(8,128)(2,1)} %bitcast.17, bf16[9,800,400]{2,1,0:T(8,128)(2,1)} %bitcast.15, s32[8,8]{1,0:T(8,128)} %neighbours.1, bf16[512,512]{1,0:T(8,128)(2,1)} %rotation.1), custom_call_target="tpu_custom_call" | custom-call | tf_op jit(solution)/shard_map/pallas_call | solution.py:277
  38.9 1.5 %shard_map.77 = (f32[512,512]{1,0:T(8,128)}, bf16[800,512]{1,0:T(8,128)(2,1)}, bf16[800,512]{1,0:T(8,128)(2,1)}) custom-call(f32[512,512]{1,0:T(8,128)S(1)} %get-tuple-element.9.refs_0_, bf16[800,512]{1,0:T(8,128)(2,1)S(1)} %get-tuple-element.10.refs_1_, bf16[800,512]{1,0:T(8,128)(2,1)S(1)} %get-tuple-element.11.refs_2_), custom_call_target="tpu_custom_call" | custom-call | tf_op jit(solution)/shard_map/pallas_call | solution.py:334

commit v4 on v3

--- a/solution.py
+++ b/solution.py
@@ -57,7 +57,7 @@
 
     barrier = pltpu.get_barrier_semaphore()
     greeted = [other] + [device(px, py, z, core) for px, py in plane] + [device(x, y, pz, c) for pz in deep for c in (core, 1 - core)]
-    greeted += [(sites[1], far)] + [(sites[k], m) for k in (4, 5) for m in (mode, far)]
+    greeted += [(sites[k], mode) for k in (4, 5)]
     for peer in greeted:
         pl.semaphore_signal(barrier, inc=1, device_id=peer, device_id_type=MESH)
 
@@ -104,7 +104,7 @@
         sent.append(copy)
 
     mine = piece.at[0, mode]
-    for k, m in ((4, far), (5, far), (4, mode), (5, mode), (2, far), (1, far), (3, far), (0, far), (2, mode), (1, mode), (3, mode)):
+    for k, m in ((0, far), (4, mode), (5, mode), (2, mode), (1, mode), (3, mode)):
         target = site if k == 0 else sites[k]
         start(remote(mine, piece.at[k, mode], halo_send.at[k, m // 2], halo_recv.at[k, mode // 2], (target, m)))
     start(remote(mine, piece.at[0, mode], forward_send.at[0, x_hi], forward_recv.at[0, x_hi], other))
@@ -129,6 +129,11 @@
             if AWAY[n] or dy:
                 py, k = (y + dy) % 4, PLANE.index((AWAY[n], dy))
                 start(remote(plane_out.at[4 * px + py], plane_in.at[k], plane_send.at[k], plane_recv.at[k], device(px, py, z, core)))
+
+    arrived(piece.at[0, far], halo_send.at[0, far // 2], halo_recv.at[0, far // 2])
+    for k in (4, 5, 2, 1, 3):
+        start(remote(piece.at[0, far], piece.at[k, far], halo_send.at[k, 1 - x_hi], halo_recv.at[k, far // 2], (sites[k], mode)))
+    start(remote(piece.at[0, far], piece.at[0, far], forward_send.at[0, far // 2], forward_recv.at[0, far // 2], other))
 
     rot_part[...] = dot(i_v[...], r_v[0:496, :], 1, 0)
 
@@ -167,9 +172,7 @@
                 term = product if term is None else term + product
             image_sum[rows, :] = term
 
-    forward(((3, mode), (1, mode), (0, far), (2, mode), (3, far), (1, far), (2, far)))
-    widen((0, 1, 2, 3))
-    loads[3].wait()
+    forward(((3, mode), (1, mode), (2, mode), (4, mode), (5, mode), (3, far), (1, far), (2, far), (4, far), (5, far)))
     for n in range(15):
         arrived(plane_in.at[n], plane_send.at[n], plane_recv.at[n])
     total = half[slot]
@@ -179,8 +182,9 @@
     for n, pz in enumerate(deep):
         start(remote(depth_buf.at[z], depth_buf.at[z], depth_send.at[n], depth_recv.at[z], device(x, y, pz, core)))
 
+    widen((0, 1, 2, 3))
+    loads[3].wait()
     stencil((0, 1, 2, 3))
-    forward(((4, mode), (5, mode), (4, far), (5, far)))
     stencil((4, 5, 6))
 
     widen((4, 5))

time: 40.6 us -> 39.1 us (0.963)
  Pallas kernels: 39.8 us -> 38.3 us
    pallas_call x1, Pallas kernels: 38.3 us -> 36.8 us  [local(): pl.pallas_call(functools.partial(kernel, scale), out_shape=(pltpu.VMEM((n...]
where the time goes in v4:
time: 39.1 us; the launch traced here: 39 us
  Pallas kernels  38.3 us (98%)
  between operations  0.64 us (2%)
    pallas_call x1, Pallas kernels, local(): pl.pallas_call(functools.partial(kernel, scale), out_shape=(pltpu.VMEM((n...  36.8 us
    pallas_call x1, Pallas kernels, local(): pl.pallas_call(finish, out_shape=(jax.ShapeDtypeStruct((nvec, nvec), F32)...  1.53 us

profile of v4, /device:TPU:1, one launch (start us, length us, event | category | flops | bytes accessed | tf_op | source)
XLA Modules:
  0.0 39.0 jit_solution(11291904209590502215)
XLA Ops:
  0.6 36.8 %shard_map.76 = (f32[512,512]{1,0:T(8,128)S(1)}, bf16[800,512]{1,0:T(8,128)(2,1)S(1)}, bf16[800,512]{1,0:T(8,128)(2,1)S(1)}) custom-call(bf16[800,512]{1,0:T(8,128)(2,1)} %bitcast.16, bf16[800,496]{1,0:T(8,128)(2,1)} %bitcast.17, bf16[9,800,400]{2,1,0:T(8,128)(2,1)} %bitcast.15, s32[8,8]{1,0:T(8,128)} %neighbours.1, bf16[512,512]{1,0:T(8,128)(2,1)} %rotation.1), custom_call_target="tpu_custom_call" | custom-call | tf_op jit(solution)/shard_map/pallas_call | solution.py:281
  37.5 1.5 %shard_map.77 = (f32[512,512]{1,0:T(8,128)}, bf16[800,512]{1,0:T(8,128)(2,1)}, bf16[800,512]{1,0:T(8,128)(2,1)}) custom-call(f32[512,512]{1,0:T(8,128)S(1)} %get-tuple-element.9.refs_0_, bf16[800,512]{1,0:T(8,128)(2,1)S(1)} %get-tuple-element.10.refs_1_, bf16[800,512]{1,0:T(8,128)(2,1)S(1)} %get-tuple-element.11.refs_2_), custom_call_target="tpu_custom_call" | custom-call | tf_op jit(solution)/shard_map/pallas_call | solution.py:338
